TPU v7x, 32 devices: a whole 2x2x4 slice. The times are simulated.
32 devices in a mesh: dp: 4 (over z), segment: 2 (over x), chan: 4 (over y, core).
Axes of the slice: x: 2, y: 2, z: 4, core: 2. Of those that a mesh axis runs over, the one named last changes fastest.
Arguments:
- base: bfloat16 [8, 512, 256], P('dp', 'chan'), may hold values from -6 to 6
- style: float32 [2, 8, 512], P('segment', 'dp'), may hold values from -3 to 3
- noise: float32 [2, 8, 256], P('segment', 'dp'), may hold values from -6 to 6
- conv_weight: bfloat16 [2, 4608, 512], P('segment', None, 'chan'), may hold values from -0.09375 to 0.09375
- conv_bias: float32 [2, 512], P('segment', 'chan'), may hold values from -3 to 3
- noise_gain: float32 [2, 512], P('segment', 'chan'), may hold values from 0.1 to 1
- rgb_weight: bfloat16 [2, 3, 512], P('segment', None, 'chan'), may hold values from -0.25 to 0.25
- disc_weight: float32 [3, 256], replicated, may hold values from -3.5 to 3.5
- disc_bias: float32 [256], replicated, may hold values from -3 to 3
- disc_out: float32 [256], replicated, may hold values from -3 to 3
Outputs:
- conv_grad: float32 [2, 4608, 512], P('segment', 'dp', 'chan')
- logits: float32 [8], P('dp')
- section_input_grads: bfloat16 [2, 8, 512, 256], P('segment', 'dp', 'chan')
All inputs are finite; a program needn't handle non-finite values.
Results may differ from a plain program's by a relative error of at most 0.015.
Values may be sent and summed in bfloat16 or wider, within the bound.
A program may use at most 64 MiB of HBM per device.

v0:
```python
import jax
import jax.numpy as jnp
from jax import lax
from jax.sharding import PartitionSpec as P

RES = 16


epsilon = 1e-06
root_two = 1.4142135623730951
highest = lax.Precision.HIGHEST
kernel_offsets = [(ky - 1, kx - 1) for ky in range(3) for kx in range(3)]


def shifted(value, axis, steps):
    count = lax.axis_size(axis)
    first, last = (max(0, -steps), min(count, count - steps))
    return lax.ppermute(value, axis, [(source, source + steps) for source in range(first, last)])


def leaky_relu(values):
    return 0.2 * values + 0.8 * jax.nn.softplus(values)


def leaky_slope(values):
    return 0.2 + 0.8 * jax.nn.sigmoid(values)


def shift_grid(values, offset_y, offset_x):
    leading = values.shape[:-1]
    planes = values.reshape(leading + (RES, RES))
    padded = jnp.pad(planes, [(0, 0)] * len(leading) + [(1, 1), (1, 1)])
    moved = padded[..., 1 + offset_y : 1 + offset_y + RES, 1 + offset_x : 1 + offset_x + RES]
    return moved.reshape(leading + (RES * RES,))


def store_slot(buffer, item, slot_clip, is_valid, axis_pos, width):
    offset = slot_clip * width
    previous = lax.dynamic_slice_in_dim(buffer, offset, width, axis_pos)
    return lax.dynamic_update_slice_in_dim(
        buffer, jnp.where(is_valid, item, previous), offset, axis_pos
    )


def shards(
    base,
    style,
    noise,
    conv_weight,
    conv_bias,
    noise_gain,
    rgb_weight,
    disc_weight,
    disc_bias,
    disc_out,
):
    weight = conv_weight[0]
    full_width = weight.shape[0] // 9
    own_width = weight.shape[1]
    micro_count = base.shape[0]
    pixels = base.shape[2]
    segment_index = lax.axis_index("segment")
    chan_index = lax.axis_index("chan")
    styles = style[0]
    own_styles = lax.dynamic_slice_in_dim(styles, chan_index * own_width, own_width, 1)
    w_float = weight.astype(jnp.float32)
    squares = jnp.sum((w_float * w_float).reshape(9, full_width, own_width), axis=0)
    style_sq = styles * styles
    demods = lax.rsqrt(
        jnp.dot(style_sq, squares, precision=highest, preferred_element_type=jnp.float32) + epsilon
    )
    bias_row = conv_bias[0]
    gain_row = noise_gain[0]
    noises = noise[0]
    rgb_proj = rgb_weight[0]
    columns_all = jnp.zeros((9 * full_width, micro_count * pixels), jnp.bfloat16)
    pre_all = jnp.zeros((micro_count, own_width, pixels), jnp.float32)
    conv_all = jnp.zeros((micro_count, own_width, pixels), jnp.float32)
    image_part = jnp.zeros((micro_count, 3, pixels), jnp.float32)
    outgoing = jnp.zeros((own_width, pixels), jnp.bfloat16)
    for tick_index in range(micro_count + 1):
        slot_index = tick_index - segment_index
        is_valid = (slot_index >= 0) & (slot_index < micro_count)
        slot_clip = jnp.clip(slot_index, 0, micro_count - 1)
        if tick_index > 0:
            incoming = shifted(outgoing, "segment", 1)
        else:
            incoming = outgoing
        first_input = lax.dynamic_index_in_dim(base, slot_clip, 0, keepdims=False)
        inputs = jnp.where(segment_index == 0, first_input, incoming)
        style_row = lax.dynamic_index_in_dim(own_styles, slot_clip, 0, keepdims=False)
        demod_row = lax.dynamic_index_in_dim(demods, slot_clip, 0, keepdims=False)
        noise_row = lax.dynamic_index_in_dim(noises, slot_clip, 0, keepdims=False)
        modulated = (inputs.astype(jnp.float32) * style_row[:, None]).astype(jnp.bfloat16)
        gathered = lax.all_gather(modulated, "chan", axis=0, tiled=True)
        columns = jnp.concatenate(
            [shift_grid(gathered, oy, ox) for oy, ox in kernel_offsets], axis=0
        )
        conv_out = lax.dot_general(
            weight, columns, (((0,), (0,)), ((), ())), preferred_element_type=jnp.float32
        )
        pre_act = (
            demod_row[:, None] * conv_out
            + gain_row[:, None] * noise_row[None, :]
            + bias_row[:, None]
        )
        out_act = (root_two * leaky_relu(pre_act)).astype(jnp.bfloat16)
        rgb_part = jnp.dot(rgb_proj, out_act, preferred_element_type=jnp.float32)
        columns_all = store_slot(columns_all, columns, slot_clip, is_valid, 1, pixels)
        pre_all = store_slot(pre_all, pre_act[None], slot_clip, is_valid, 0, 1)
        conv_all = store_slot(conv_all, conv_out[None], slot_clip, is_valid, 0, 1)
        image_part = store_slot(image_part, rgb_part[None], slot_clip, is_valid, 0, 1)
        outgoing = out_act
    images = lax.psum(image_part, ("segment", "chan"))
    pre_disc = (
        jnp.einsum("cj,mcp->mjp", disc_weight, images, precision=highest) + disc_bias[None, :, None]
    )
    hidden = leaky_relu(pre_disc)
    logits = jnp.dot(
        jnp.mean(hidden, axis=2), disc_out, precision=highest, preferred_element_type=jnp.float32
    )
    grad_logit = jax.nn.sigmoid(logits) - 1.0
    d_pre = grad_logit[:, None, None] * disc_out[None, :, None] / pixels * leaky_slope(pre_disc)
    d_image = jnp.einsum("cj,mjp->mcp", disc_weight, d_pre, precision=highest)
    head_grad = jnp.einsum("co,mcp->mop", rgb_proj.astype(jnp.float32), d_image, precision=highest)
    grads_all = jnp.zeros((own_width, micro_count * pixels), jnp.bfloat16)
    coef_all = jnp.zeros((micro_count, own_width), jnp.float32)
    returned_all = jnp.zeros((micro_count, own_width, pixels), jnp.bfloat16)
    returned = jnp.zeros((own_width, pixels), jnp.bfloat16)
    for tick_index in range(micro_count + 1):
        slot_index = tick_index - 1 + segment_index
        is_valid = (slot_index >= 0) & (slot_index < micro_count)
        slot_clip = jnp.clip(slot_index, 0, micro_count - 1)
        if tick_index > 0:
            incoming = shifted(returned, "segment", -1)
        else:
            incoming = returned
        style_row = lax.dynamic_index_in_dim(own_styles, slot_clip, 0, keepdims=False)
        demod_row = lax.dynamic_index_in_dim(demods, slot_clip, 0, keepdims=False)
        pre_act = lax.dynamic_index_in_dim(pre_all, slot_clip, 0, keepdims=False)
        conv_out = lax.dynamic_index_in_dim(conv_all, slot_clip, 0, keepdims=False)
        grad_out = lax.dynamic_index_in_dim(
            head_grad, slot_clip, 0, keepdims=False
        ) + incoming.astype(jnp.float32)
        d_act = grad_out * root_two * leaky_slope(pre_act)
        d_conv = (d_act * demod_row[:, None]).astype(jnp.bfloat16)
        d_demod = jnp.sum(d_act * conv_out, axis=1)
        coef_row = -d_demod * demod_row * demod_row * demod_row
        grads_all = store_slot(grads_all, d_conv, slot_clip, is_valid, 1, pixels)
        coef_all = store_slot(coef_all, coef_row[None], slot_clip, is_valid, 0, 1)
        total = jnp.zeros((own_width * lax.axis_size("chan"), pixels), jnp.float32)
        for kernel_pos, (input_oy, input_ox) in enumerate(kernel_offsets):
            weight_rows = lax.dynamic_slice_in_dim(
                weight, kernel_pos * full_width, own_width * lax.axis_size("chan"), 0
            )
            piece_out = lax.dot_general(
                weight_rows, d_conv, (((1,), (0,)), ((), ())), preferred_element_type=jnp.float32
            )
            total = total + shift_grid(piece_out, -input_oy, -input_ox)
        d_input = lax.psum_scatter(total, "chan", scatter_dimension=0, tiled=True)
        returned = (d_input * style_row[:, None]).astype(jnp.bfloat16)
        returned_all = store_slot(returned_all, returned[None], slot_clip, is_valid, 0, 1)
    demod_total = jnp.dot(
        style_sq.T, coef_all, precision=highest, preferred_element_type=jnp.float32
    )
    demod_term = (w_float.reshape(9, full_width, own_width) * demod_total[None]).reshape(
        9 * full_width, own_width
    )
    local_grad = lax.dot_general(
        columns_all, grads_all, (((1,), (1,)), ((), ())), preferred_element_type=jnp.float32
    )
    grad_rows = lax.psum_scatter(
        (local_grad + demod_term).astype(jnp.bfloat16), "dp", scatter_dimension=0, tiled=True
    ).astype(jnp.float32)
    return (grad_rows[None], logits, returned_all[None])


def solution(mesh):
    placed = (
        P("dp", "chan", None),
        P("segment", "dp", None),
        P("segment", "dp", None),
        P("segment", None, "chan"),
        P("segment", "chan"),
        P("segment", "chan"),
        P("segment", None, "chan"),
        P(),
        P(),
        P(),
    )
    return jax.shard_map(
        shards,
        mesh=mesh,
        in_specs=placed,
        out_specs=(P("segment", "dp", "chan"), P("dp"), P("segment", "dp", "chan", None)),
        check_vma=False,
    )
```

profile of v0, /device:TPU:0, one launch (start us, length us, event | category | flops | bytes accessed | tf_op | source)
XLA Modules:
  0.0 225.6 jit_solution(7355478076075970710)
XLA Ops:
  7.3 1.6 constant_dynamic-slice_fusion.15
  9.0 1.6 fusion.192
  10.6 7.2 %all_gather.9 = bf16[512,256]{0,1:T(8,128)(2,1)S(1)} all-gather(bf16[128,256]{0,1:T(8,128)(2,1)S(1)} %fusion.71), channel_id=1, replica_groups=mesh['dp'=4,'segment'=2,'chan'=4] {'chan'}, dimensions={0}, use_global_device_ids=true | all-gather | bytes 327680 | tf_op jit(solution)/shard_map/all_gather | solution.py:95
  17.8 1.2 pad_slice_fusion.40
  19.5 1.6 convert_multiply_fusion
  21.1 2.5 %reduce_sum.45 = f32[512,128]{1,0:T(8,128)} reduce(f32[9,512,128]{2,1,0:T(8,128)} %bitcast.491, f32[]{:T(128)} %constant.228.clone.1), dimensions={0}, to_apply=%region_0.0 | reduce | flops 524288 | bytes 2621444 | tf_op jit(solution)/shard_map/reduce_sum | solution.py:67
  23.6 1.2 fusion.29
  26.9 1.0 constant_dynamic-update-slice_fusion.2
  27.9 1.0 constant_dynamic-update-slice_fusion.1
  28.9 1.0 constant_dynamic-update-slice_fusion
  30.6 1.5 bitcast_dynamic-update-slice_fusion
  32.1 1.4 fusion.56
  33.5 4.0 %collective-permute-start = (bf16[128,256]{0,1:T(8,128)(2,1)}, bf16[128,256]{0,1:T(8,128)(2,1)}, u32[]{:S(2)}, u32[]{:S(2)}) collective-permute-start(bf16[128,256]{0,1:T(8,128)(2,1)} %fusion.56), channel_id=1, source_target_pairs={{0,4},{1,5},{2,6},{3,7},{8,12},{9,13},{10,14},{11,15},{16,20},{17,... | collective-permute-start | bytes 196616 | tf_op jit(solution)/shard_map/ppermute | solution.py:18
  39.0 1.0 fusion.28
  40.0 1.6 copy.14
  41.6 1.6 copy.15
  44.0 5.8 %all_gather.10 = bf16[512,256]{0,1:T(8,128)(2,1)S(1)} all-gather(bf16[128,256]{0,1:T(8,128)(2,1)S(1)} %multiply_convert_fusion.7), channel_id=1, replica_groups=mesh['dp'=4,'segment'=2,'chan'=4] {'chan'}, dimensions={0}, use_global_device_ids=true | all-gather | bytes 327680 | tf_op jit(solution)/shard_map/all_gather | solution.py:95
  50.8 2.8 %fusion.66 = (f32[2,128,256]{1,2,0:T(8,128)}, f32[2,128,256]{1,2,0:T(8,128)}, f32[256,128]{1,0:T(8,128)S(1)}) fusion(f32[2,128,256]{1,2,0:T(8,128)} %get-tuple-element.67, s32[]{:T(128)S(6)} %min.33, pred[]{:T(512)S(6)} %and.21, f32[2,128,256]{1,2,0:T(8,128)} %bitcast_dynamic-update-slice_fusion.1, f32[128]{0:T(128)S(1)} %bitcast.564, ...), kind=kOutput, calls=%fused_computation.137 | convolution fusion | flops 302186496 | bytes 4196869 | tf_op jit(solution)/shard_map/dot_general | solution.py:99
  53.8 1.3 collective-permute-start.1
  55.2 2.0 collective-permute-done.1
  57.2 5.8 %all_gather.11 = bf16[512,256]{0,1:T(8,128)(2,1)S(1)} all-gather(bf16[128,256]{0,1:T(8,128)(2,1)S(1)} %multiply_convert_fusion.6), channel_id=1, replica_groups=mesh['dp'=4,'segment'=2,'chan'=4] {'chan'}, dimensions={0}, use_global_device_ids=true | all-gather | bytes 327680 | tf_op jit(solution)/shard_map/all_gather | solution.py:95
  63.6 1.4 copy-done.4
  65.1 2.5 %fusion.65 = (f32[2,128,256]{1,2,0:T(8,128)}, f32[2,128,256]{1,2,0:T(8,128)}, f32[256,128]{1,0:T(8,128)S(1)}) fusion(f32[2,128,256]{1,2,0:T(8,128)} %get-tuple-element.47, s32[]{:T(128)S(6)} %min.35, pred[]{:T(512)S(6)} %and.22, f32[2,128,256]{1,2,0:T(8,128)} %get-tuple-element.48, f32[128]{0:T(128)S(1)} %bitcast.566, f32[256]{0:T(256)S(1)} %bitcast.560, ...), kind=kOutput, calls=%fused_computation.135 | convolution fusion | flops 302186496 | bytes 4196869 | tf_op jit(solution)/shard_map/dot_general | solution.py:99
  67.8 16.0 %psum.7 = f32[2,3,256]{2,1,0:T(4,128)} all-reduce(f32[2,3,256]{2,1,0:T(4,128)S(1)} %fusion.26), channel_id=1, replica_groups=mesh['dp'=4,'segment'=2,'chan'=4] {'segment','chan'}, use_global_device_ids=true, to_apply=%region_1.2 | all-reduce | flops 1536 | bytes 12288 | tf_op jit(solution)/shard_map/psum | solution.py:114
  83.8 1.6 fusion.41
  85.5 1.3 divide_add_fusion
  88.7 1.1 fusion.167
  92.1 1.1 fusion.8
  93.3 21.1 %reduce-scatter.5.cloned.1.call-done = f32[128,256]{0,1:T(8,128)} async-done(((f32[512,256]{0,1:T(8,128)}), f32[128,256]{0,1:T(8,128)}) %reduce-scatter.5.cloned.1.call-update) | async-done | bytes 131088 | tf_op jit(solution)/shard_map/reduce_scatter | solution.py:160
  115.1 1.6 bitcast_dynamic-update-slice_fusion.2
  116.6 1.5 collective-permute-start.2
  118.1 2.4 %broadcast_in_dim.35 = bf16[4608,512]{0,1:T(8,128)(2,1)} broadcast(bf16[]{:T(256)} %constant.217.clone.1), dimensions={} | broadcast | bytes 4718594 | tf_op jit(solution)/shard_map/broadcast_in_dim | solution.py:76
  120.5 1.8 select_dynamic-update-slice_fusion.2
  123.1 1.8 select_dynamic-update-slice_fusion.4
  127.2 1.1 fusion.12
  129.0 3.7 %select_dynamic-update-slice_fusion.1 = bf16[4608,512]{0,1:T(8,128)(2,1)} fusion(bf16[4608,512]{0,1:T(8,128)(2,1)} %select_dynamic-update-slice_fusion.2, s32[]{:T(128)S(6)} %select_n.277, bf16[4608,256]{0,1:T(8,128)(2,1)S(1)} %copy-done.3, pred[]{:T(512)S(6)} %and.21), kind=kLoop, calls=%fused_computation.4 | loop fusion | flops 1179648 | bytes 7077893 | tf_op jit(solution)/shard_map/dynamic_update_slice | solution.py:40
  132.8 18.2 %reduce-scatter.7.cloned.1.call-done = f32[128,256]{0,1:T(8,128)} async-done(((f32[512,256]{0,1:T(8,128)}), f32[128,256]{0,1:T(8,128)}) %reduce-scatter.7.cloned.1.call-update) | async-done | bytes 131088 | tf_op jit(solution)/shard_map/reduce_scatter | solution.py:160
  150.9 1.6 fusion.168
  152.5 1.4 collective-permute-start.3
  153.9 3.6 %select_dynamic-update-slice_fusion = bf16[4608,512]{0,1:T(8,128)(2,1)} fusion(bf16[4608,512]{0,1:T(8,128)(2,1)} %select_dynamic-update-slice_fusion.1, s32[]{:T(128)S(6)} %select_n.282, bf16[4608,256]{0,1:T(8,128)(2,1)} %copy-done.4, pred[]{:T(512)S(6)} %and.22), kind=kLoop, calls=%fused_computation.3 | loop fusion | flops 1179648 | bytes 7077893 | tf_op jit(solution)/shard_map/dynamic_update_slice | solution.py:40
  157.6 1.2 collective-permute-done.3
  158.8 1.0 select_dynamic-update-slice_fusion.3
  162.2 1.1 fusion.16
  163.3 1.1 fusion.72
  165.5 4.9 %fusion = bf16[4608,128]{1,0:T(8,128)(2,1)} fusion(f32[4608,128]{1,0:T(8,128)S(1)} %bitcast_multiply_fusion, bf16[4608,512]{0,1:T(8,128)(2,1)} %select_dynamic-update-slice_fusion, bf16[128,512]{0,1:T(8,128)(2,1)S(1)} %get-tuple-element.13), kind=kOutput, calls=%fused_computation.1 | convolution fusion | flops 605159424 | bytes 8388608 | tf_op jit(solution)/shard_map/dot_general | solution.py:169
  171.3 14.5 %reduce-scatter.11.cloned.1.call-done = f32[128,256]{0,1:T(8,128)} async-done(((f32[512,256]{0,1:T(8,128)}), f32[128,256]{0,1:T(8,128)}) %reduce-scatter.11.cloned.1.call-update) | async-done | bytes 131088 | tf_op jit(solution)/shard_map/reduce_scatter | solution.py:160
  187.5 29.8 %reduce-scatter.9.cloned.1.call-done = bf16[1152,128]{1,0:T(8,128)(2,1)} async-done(((bf16[4608,128]{1,0:T(8,128)(2,1)}), bf16[1152,128]{1,0:T(8,128)(2,1)}) %reduce-scatter.9.cloned.1.call-update) | async-done | bytes 294928 | tf_op jit(solution)/shard_map/reduce_scatter | solution.py:172
  217.3 1.8 bitcast_convert_fusion
  (179 shorter events, 22.3 us)
Async XLA Ops:
  7.2 76.6 %copy-start = (f32[3,256]{1,0:T(4,128)S(1)}, f32[3,256]{1,0:T(4,128)}, u32[]{:S(2)}) copy-start(f32[3,256]{1,0:T(4,128)} %param.17) | copy-start | bytes 9220
  7.2 107.2 %reduce-scatter.5.cloned.1.call-start = ((), (), s32[]{:S(2)}) async-start(), calls=%async_computation.4 | async-start | bytes 655360 | tf_op jit(solution)/shard_map/reduce_scatter | solution.py:160
  17.8 1.6 copy-start.1
  19.5 4.1 %copy-start.13 = (f32[1,2,512]{2,1,0:T(2,128)S(1)}, f32[1,2,512]{2,1,0:T(2,128)}, u32[]{:S(2)}) copy-start(f32[1,2,512]{2,1,0:T(2,128)} %param.11) | copy-start | bytes 12292
  19.5 5.9 %copy-start.29 = (f32[1,2,256]{2,1,0:T(2,128)S(1)}, f32[1,2,256]{2,1,0:T(2,128)}, u32[]{:S(2)}) copy-start(f32[1,2,256]{2,1,0:T(2,128)} %param.12) | copy-start | bytes 6148
  24.7 4.1 %copy-start.15 = (f32[2,128]{1,0:T(2,128)}, f32[2,128]{1,0:T(2,128)S(1)}, u32[]{:S(2)}) copy-start(f32[2,128]{1,0:T(2,128)S(1)} %fusion.29) | copy-start | bytes 3076
  28.8 3.2 %copy-start.18 = (f32[1,128]{1,0:T(1,128)S(1)}, f32[1,128]{1,0:T(1,128)}, u32[]{:S(2)}) copy-start(f32[1,128]{1,0:T(1,128)} %param.14) | copy-start | bytes 1540
  28.9 3.2 %copy-start.20 = (f32[1,128]{1,0:T(1,128)S(1)}, f32[1,128]{1,0:T(1,128)}, u32[]{:S(2)}) copy-start(f32[1,128]{1,0:T(1,128)} %param.15) | copy-start | bytes 1540
  29.9 8.4 %copy-start.25 = (f32[1,1,256]{2,1,0:T(1,128)S(1)}, f32[1,1,256]{2,1,0:T(1,128)}, u32[]{:S(2)}) copy-start(f32[1,1,256]{2,1,0:T(1,128)} %get-tuple-element.59) | copy-start | bytes 3076
  29.9 8.4 %copy-start.28 = (f32[128]{0:T(128)S(1)}, f32[128]{0:T(128)}, u32[]{:S(2)}) copy-start(f32[128]{0:T(128)} %get-tuple-element.66) | copy-start | bytes 1540
  29.9 9.2 %copy-start.22 = (bf16[1,3,128]{2,1,0:T(4,128)(2,1)S(1)}, bf16[1,3,128]{2,1,0:T(4,128)(2,1)}, u32[]{:S(2)}) copy-start(bf16[1,3,128]{2,1,0:T(4,128)(2,1)} %param.16) | copy-start | bytes 2308
  33.5 9.6 %collective-permute-start = (bf16[128,256]{0,1:T(8,128)(2,1)}, bf16[128,256]{0,1:T(8,128)(2,1)}, u32[]{:S(2)}, u32[]{:S(2)}) collective-permute-start(bf16[128,256]{0,1:T(8,128)(2,1)} %fusion.56), channel_id=1, source_target_pairs={{0,4},{1,5},{2,6},{3,7},{8,12},{9,13},{10,14},{11,15},{16,20},{17,... | collective-permute-start | bytes 196616 | tf_op jit(solution)/shard_map/ppermute | solution.py:18
  50.1 0.7 copy-start.19
  50.1 0.7 copy-start.21
  50.2 0.7 copy-start.26
  50.4 4.7 %copy-start.23 = (bf16[1,3,128]{2,1,0:T(4,128)(2,1)S(1)}, bf16[1,3,128]{2,1,0:T(4,128)(2,1)}, u32[]{:S(2)}) copy-start(bf16[1,3,128]{2,1,0:T(4,128)(2,1)} %param.16) | copy-start | bytes 2308
  50.4 12.6 %copy-start.2 = (bf16[4608,256]{0,1:T(8,128)(2,1)}, bf16[4608,256]{0,1:T(8,128)(2,1)S(1)}, u32[]{:S(2)}) copy-start(bf16[4608,256]{0,1:T(8,128)(2,1)S(1)} %constant_dynamic-update-slice_fusion.9) | copy-start | bytes 7077892
  50.4 6.8 %copy-start.12 = (bf16[1,128,256]{1,2,0:T(8,128)(2,1)S(1)}, bf16[1,128,256]{1,2,0:T(8,128)(2,1)}, u32[]{:S(2)}) copy-start(bf16[1,128,256]{1,2,0:T(8,128)(2,1)} %copy.15) | copy-start | bytes 196612
  50.4 6.8 %copy-start.36 = (f32[128]{0:T(128)S(1)}, f32[128]{0:T(128)}, u32[]{:S(2)}) copy-start(f32[128]{0:T(128)} %get-tuple-element.54) | copy-start | bytes 1540
  53.8 3.4 %collective-permute-start.1 = (bf16[128,256]{0,1:T(8,128)(2,1)S(1)}, bf16[128,256]{0,1:T(8,128)(2,1)S(1)}, u32[]{:S(2)}, u32[]{:S(2)}) collective-permute-start(bf16[128,256]{0,1:T(8,128)(2,1)S(1)} %fusion.60), channel_id=1, source_target_pairs={{0,4},{1,5},{2,6},{3,7},{8,12},{9,13},{10,14},{11,15},{16,20},{17,... | collective-permute-start | bytes 196616 | tf_op jit(solution)/shard_map/ppermute | solution.py:18
  63.3 1.7 copy-start.17
  63.3 1.7 copy-start.30
  63.6 1.5 copy-start.4
  67.5 20.7 %copy-start.24 = (bf16[1,3,128]{2,1,0:T(4,128)(2,1)S(1)}, bf16[1,3,128]{2,1,0:T(4,128)(2,1)}, u32[]{:S(2)}) copy-start(bf16[1,3,128]{2,1,0:T(4,128)(2,1)} %param.16) | copy-start | bytes 2308
  83.8 4.9 %copy-start.27 = (f32[128]{0:T(128)S(1)}, f32[128]{0:T(128)}, u32[]{:S(2)}) copy-start(f32[128]{0:T(128)} %get-tuple-element.63) | copy-start | bytes 1540
  88.6 2.5 %copy-start.5 = (f32[2,256,128]{2,1,0:T(8,128)}, f32[2,256,128]{2,1,0:T(8,128)S(1)}, u32[]{:S(2)}) copy-start(f32[2,256,128]{2,1,0:T(8,128)S(1)} %fusion.178) | copy-start | bytes 786436
  89.7 1.7 copy-start.7
  89.7 1.7 copy-start.9
  92.1 22.9 %copy-start.35 = (f32[128]{0:T(128)S(1)}, f32[128]{0:T(128)}, u32[]{:S(2)}) copy-start(f32[128]{0:T(128)} %get-tuple-element.53) | copy-start | bytes 1540
  93.2 57.7 %reduce-scatter.7.cloned.1.call-start = ((), (), s32[]{:S(2)}) async-start(), calls=%async_computation.5 | async-start | bytes 655360 | tf_op jit(solution)/shard_map/reduce_scatter | solution.py:160
  116.6 6.5 %collective-permute-start.2 = (bf16[128,256]{0,1:T(8,128)(2,1)}, bf16[128,256]{0,1:T(8,128)(2,1)}, u32[]{:S(2)}, u32[]{:S(2)}) collective-permute-start(bf16[128,256]{0,1:T(8,128)(2,1)} %get-tuple-element.12), channel_id=1, source_target_pairs={{4,0},{5,1},{6,2},{7,3},{12,8},{13,9},{14,10},{15,11},{20,16},{21,... | collective-permute-start | bytes 196616 | tf_op jit(solution)/shard_map/ppermute | solution.py:18
  120.5 2.6 %copy-start.34 = (f32[128]{0:T(128)S(1)}, f32[128]{0:T(128)}, u32[]{:S(2)}) copy-start(f32[128]{0:T(128)} %get-tuple-element.62) | copy-start | bytes 1540
  127.2 1.9 copy-start.3
  128.3 22.7 %copy-start.32 = (f32[128]{0:T(128)S(1)}, f32[128]{0:T(128)}, u32[]{:S(2)}) copy-start(f32[128]{0:T(128)} %get-tuple-element.57) | copy-start | bytes 1540
  128.3 57.5 %reduce-scatter.11.cloned.1.call-start = ((), (), s32[]{:S(2)}) async-start(), calls=%async_computation.7 | async-start | bytes 655360 | tf_op jit(solution)/shard_map/reduce_scatter | solution.py:160
  152.5 6.3 %copy-start.6 = (f32[2,256,128]{2,1,0:T(8,128)S(1)}, f32[2,256,128]{2,1,0:T(8,128)}, u32[]{:S(2)}) copy-start(f32[2,256,128]{2,1,0:T(8,128)} %copy-done.5) | copy-start | bytes 786436
  152.5 6.3 %copy-start.8 = (bf16[128,512]{0,1:T(8,128)(2,1)S(1)}, bf16[128,512]{0,1:T(8,128)(2,1)}, u32[]{:S(2)}) copy-start(bf16[128,512]{0,1:T(8,128)(2,1)} %get-tuple-element.16) | copy-start | bytes 393220
  152.5 6.3 %copy-start.33 = (f32[128]{0:T(128)S(1)}, f32[128]{0:T(128)}, u32[]{:S(2)}) copy-start(f32[128]{0:T(128)} %get-tuple-element.61) | copy-start | bytes 1540
  152.5 6.3 %collective-permute-start.3 = (bf16[128,256]{0,1:T(8,128)(2,1)S(1)}, bf16[128,256]{0,1:T(8,128)(2,1)S(1)}, u32[]{:S(2)}, u32[]{:S(2)}) collective-permute-start(bf16[128,256]{0,1:T(8,128)(2,1)S(1)} %get-tuple-element.10), channel_id=1, source_target_pairs={{4,0},{5,1},{6,2},{7,3},{12,8},{13,9},{14,10},{15,11},{20,16},{21,... | collective-permute-start | bytes 196616 | tf_op jit(solution)/shard_map/ppermute | solution.py:18
  162.1 1.2 copy-start.10
  162.1 1.2 copy-start.11
  162.2 2.3 %copy-start.16 = (f32[2,128]{1,0:T(2,128)S(1)}, f32[2,128]{1,0:T(2,128)}, u32[]{:S(2)}) copy-start(f32[2,128]{1,0:T(2,128)} %copy-done.15) | copy-start | bytes 3076
  162.2 2.5 %copy-start.14 = (f32[1,2,512]{2,1,0:T(2,128)S(1)}, f32[1,2,512]{2,1,0:T(2,128)}, u32[]{:S(2)}) copy-start(f32[1,2,512]{2,1,0:T(2,128)} %param.11) | copy-start | bytes 12292
  163.3 54.0 %reduce-scatter.9.cloned.1.call-start = ((), (), s32[]{:S(2)}) async-start(), calls=%async_computation.6 | async-start | bytes 1474560 | tf_op jit(solution)/shard_map/reduce_scatter | solution.py:172
  165.4 20.3 %copy-start.31 = (f32[128]{0:T(128)S(1)}, f32[128]{0:T(128)}, u32[]{:S(2)}) copy-start(f32[128]{0:T(128)} %get-tuple-element.52) | copy-start | bytes 1540
Sparse Core Ops, SparseCore 0:
  93.3 20.9 reduce-scatter.4
  128.4 22.5 reduce-scatter.6
  163.4 22.3 reduce-scatter.10
  188.1 29.1 reduce-scatter.8
where the time goes:
time: 227 us; the launch traced here: 226 us
  waiting for transfers between devices  87.5 us (39%)
  blocking collectives  34.8 us (15%)
  other arithmetic  29.1 us (13%)
  matrix products  27.4 us (12%)
  local copies, waits for them, and re-layouts  23.6 us (10%)
  between operations  14.8 us (7%)
  starting transfers between devices  8.37 us (4%)
    reduce_scatter x3, waiting for transfers between devices, shards(): d_input = lax.psum_scatter(total, 'chan', scatter_dimension=0, tiled=True)  53.8 us
    reduce_scatter x1, waiting for transfers between devices, shards(): lax.psum_scatter((local_grad + demod_term).astype(jnp.bfloat16), 'dp', sc...  29.8 us
    all_gather x3, blocking collectives, shards(): gathered = lax.all_gather(modulated, 'chan', axis=0, tiled=True)  18.9 us
    dynamic_update_slice x10, other arithmetic, store_slot(): lax.dynamic_update_slice_in_dim(buffer, jnp.where(is_valid, item, previou...  17.8 us
    psum x1, blocking collectives, shards(): images = lax.psum(image_part, ('segment', 'chan'))  16 us
    dot_general x27, matrix products, shards(): lax.dot_general(weight_rows, d_conv, (((1,), (0,)), ((), ())), preferred_...  8.59 us
    ppermute x4, starting transfers between devices, shifted(): lax.ppermute(value, axis, [(source, source + steps) for source in range(f...  8.21 us
    unnamed x101, local copies, waits for them, and re-layouts  8.12 us
  transfers between devices with their start and end apart: 8, of which 7 were waited for; matrix products, arithmetic and copies ran while one was open for 12% of the time, Pallas kernels for 0%

commit v1 on v0

v1 whole, which is shorter than its diff:
```python
import functools
import math
import jax
import jax.numpy as jnp
from jax import lax
from jax.experimental import pallas as pl
from jax.experimental.pallas import tpu as pltpu
from jax.sharding import PartitionSpec as P

epsilon = 1e-06
root_two = 1.4142135623730951
f32 = jnp.float32
bf16 = jnp.bfloat16
MESH = pl.DeviceIdType.MESH
OFFSETS = [(ky - 1, kx - 1) for ky in range(3) for kx in range(3)]


def leaky_pair(t):
    e = jnp.exp(-jnp.abs(t))
    act = 0.2 * t + 0.8 * (jnp.maximum(t, 0.0) + jnp.log1p(e))
    slope = 0.2 + 0.8 * (jnp.where(t >= 0.0, 1.0, e) / (1.0 + e))
    return act, slope


def remote(src, dst, send_sem, recv_sem, dev):
    return pltpu.make_async_remote_copy(
        src_ref=src,
        dst_ref=dst,
        send_sem=send_sem,
        recv_sem=recv_sem,
        device_id=dev,
        device_id_type=MESH,
    )


def kernel(
    nd,
    nc,
    base_ref,
    style_ref,
    noise_ref,
    w_ref,
    bias_ref,
    gain_ref,
    rgb_ref,
    dw_ref,
    db_ref,
    do_ref,
    grad_out,
    logit_out,
    ret_out,
    pack,
    cols,
    dpack,
    dcols,
    wt,
    wcat,
    demods,
    yin,
    ytx,
    xfull,
    styall,
    coefall,
    conv_s,
    pre_s,
    img,
    dimg,
    gzall,
    gst,
    tx,
    rx,
    dxown,
    retbuf,
    rettx,
    gt,
    dmat,
    xg_s,
    xg_r,
    xd_s,
    xd_r,
    xf_s,
    xf_r,
    im_s,
    im_r,
    yy_s,
    yy_r,
    rs_s,
    rs_r,
    rt_s,
    rt_r,
    gz_s,
    gz_r,
    cf_s,
    cf_r,
    st_s,
    st_r,
):
    dp = lax.axis_index("dp")
    seg = lax.axis_index("segment")
    ch = lax.axis_index("chan")
    mb, ow, px = base_ref.shape
    full = w_ref.shape[1] // 9
    res = math.isqrt(px)
    nb = nd * mb
    ng = 2 * nc

    def at(d, s, c):
        return {"dp": d, "segment": s, "chan": c}

    def chan_peer(j):
        return lax.rem(ch + j, nc)

    def chan_from(j):
        return lax.rem(ch + nc - j, nc)

    def dp_peer(j):
        return lax.rem(dp + j, nd)

    def dp_from(j):
        return lax.rem(dp + nd - j, nd)

    me_group = seg * nc + ch

    barrier = pltpu.get_barrier_semaphore()
    for j in range(1, ng):
        g = lax.rem(me_group + j, ng)
        pl.semaphore_signal(
            barrier, inc=1, device_id=at(dp, g // nc, lax.rem(g, nc)), device_id_type=MESH
        )
    for j in range(1, nd):
        pl.semaphore_signal(barrier, inc=1, device_id=at(dp_peer(j), seg, ch), device_id_type=MESH)

    pack[...] = jnp.zeros_like(pack)
    pack[0:3, :] = rgb_ref[0].astype(f32)
    pack[3:4, :] = bias_ref[...]
    pack[4:5, :] = gain_ref[...]
    pack[5 : 5 + mb, :] = style_ref[0, :, pl.ds(pl.multiple_of(ch * ow, ow), ow)]
    cols[...] = pack[...].T

    def own_x(d, m):
        return xfull.at[
            pl.ds(pl.multiple_of(ch * ow, ow), ow),
            pl.ds(pl.multiple_of((d * mb + m) * px, px), px),
        ]

    def x_block(d, m, c, n=1):
        return xfull.at[
            pl.ds(pl.multiple_of(c * ow, ow), ow),
            pl.ds(pl.multiple_of((d * mb + m) * px, px), n * px),
        ]

    pairs = nc // 2
    pair, core = ch // 2, lax.rem(ch, 2)
    other = pair * 2 + 1 - core

    def same_core(q):
        return lax.rem(pair + q, pairs) * 2 + core

    def came_from(q, c):
        return lax.rem(pair + pairs - q, pairs) * 2 + c

    def gather_out(block, sends, recvs):
        ops = [remote(block(ch), block(ch), sends(q), recvs(q), at(dp, seg, same_core(q)))
               for q in range(1, pairs)]
        return ops + [remote(block(ch), block(ch), sends(0), recvs(0), at(dp, seg, other))]

    def gather_relay(block, sends, recvs):
        ops = []
        for q in range(1, pairs):
            i = pairs - 1 + q
            ref = block(came_from(q, core))
            ops.append(remote(ref, ref, sends(i), recvs(i), at(dp, seg, other)))
        return ops

    def relay_in(block, sends, recvs):
        ops = []
        for q in range(1, pairs):
            ref = block(came_from(q, core))
            ops.append(remote(ref, ref, sends(q), recvs(q), at(dp, seg, other)))
        return ops

    def gather_in(block, sends, recvs):
        ops = [remote(block(other), block(other), sends(0), recvs(0), at(dp, seg, other))]
        for q in range(1, pairs):
            i = pairs - 1 + q
            ref = block(came_from(q, 1 - core))
            ops.append(remote(ref, ref, sends(i), recvs(i), at(dp, seg, other)))
        return ops

    def of_sample(m):
        return (
            lambda c: x_block(dp, m, c),
            lambda i: xg_s.at[m, i],
            lambda i: xg_r.at[m, i],
        )

    def of_dp(jd):
        return (
            lambda c: x_block(dp_from(jd), 0, c, mb),
            lambda i: xf_s.at[jd - 1, i],
            lambda i: xf_r.at[jd - 1, i],
        )

    def relay(group):
        for op in relay_in(*group):
            op.wait_recv()
        for op in gather_relay(*group):
            op.start()

    def x_dp(m, j):
        ref = x_block(dp, m, ch)
        return remote(ref, ref, xd_s.at[m, j - 1], xd_r.at[m, j - 1], at(dp_peer(j), seg, ch))

    def x_dp_in(m, j):
        ref = x_block(dp_from(j), m, ch)
        return remote(ref, ref, xd_s.at[m, j - 1], xd_r.at[m, j - 1], at(dp_peer(j), seg, ch))

    def style_dp(j, source):
        ref = styall.at[source]
        return remote(ref, ref, st_s.at[j - 1], st_r.at[j - 1], at(dp_peer(j), seg, ch))

    def coef_dp(j, source):
        ref = coefall.at[source]
        return remote(ref, ref, cf_s.at[j - 1], cf_r.at[j - 1], at(dp_peer(j), seg, ch))

    def image_copy(m, j, source):
        g = lax.rem(me_group + j, ng)
        ref = img.at[m, source]
        return remote(
            ref, ref, im_s.at[m, j - 1], im_r.at[m, j - 1], at(dp, g // nc, lax.rem(g, nc))
        )

    def y_copy(m):
        return remote(ytx.at[m], yin.at[m], yy_s.at[m], yy_r.at[m], at(dp, 1 - seg, ch))

    def ret_copy(m):
        return remote(rettx.at[m], retbuf.at[m], rt_s.at[m], rt_r.at[m], at(dp, 1 - seg, ch))

    def dx_copy(m, j):
        return remote(
            tx.at[m, j - 1],
            rx.at[m, j - 1],
            rs_s.at[m, j - 1],
            rs_r.at[m, j - 1],
            at(dp, seg, chan_peer(j)),
        )

    def gz_block(d, m):
        return gzall.at[:, pl.ds(pl.multiple_of((d * mb + m) * px, px), px)]

    def gz_copy(m, j, source):
        ref = gz_block(source, m)
        return remote(ref, ref, gz_s.at[m, j - 1], gz_r.at[m, j - 1], at(dp_peer(j), seg, ch))

    def send_x(m, value):
        style_col = cols[:, 5 + m : 6 + m]
        own_x(dp, m)[...] = (value.astype(f32) * style_col).astype(bf16)
        for op in gather_out(*of_sample(m)):
            op.start()

    styall[dp] = jnp.zeros((styall.shape[1], full), f32)
    styall[dp, 0:mb, :] = style_ref[0]
    pl.semaphore_wait(barrier, ng - 1 + nd - 1)

    @pl.when(seg == 0)
    def _():
        for m in range(mb):
            send_x(m, base_ref[m])
        for m in range(mb):
            for j in range(1, nd):
                x_dp(m, j).start()

    for j in range(1, nd):
        style_dp(j, dp).start()

    squares = jnp.zeros((ow, full), f32)
    for k in range(9):
        if k == 5:

            @pl.when(seg == 0)
            def _():
                for m in range(mb):
                    relay(of_sample(m))

        block = w_ref[0, k * full : (k + 1) * full, :]
        wcat[:, k * ow : (k + 1) * ow] = block
        turned = block.T
        wt[k * ow : (k + 1) * ow, :] = turned
        wide = turned.astype(f32)
        squares = squares + wide * wide
    for m in range(mb):
        row = style_ref[0, m : m + 1, :]
        total = jnp.sum(squares * (row * row), axis=1, keepdims=True)
        demods[:, m : m + 1] = lax.rsqrt(total + epsilon)
    dpack[...] = jnp.zeros_like(dpack)
    dpack[0:3, :] = dw_ref[...]
    dpack[3:4, :] = db_ref[...]
    dpack[4:5, :] = do_ref[...]
    dcols[...] = dpack[...].T

    @pl.when(seg == 1)
    def _():
        retbuf[...] = jnp.zeros_like(retbuf)
        for m in range(mb):
            y_copy(m).wait_recv()
            send_x(m, yin[m])
        for m in range(mb):
            relay(of_sample(m))
        for m in range(mb):
            for j in range(1, nd):
                x_dp(m, j).start()

    lane = lax.broadcasted_iota(jnp.int32, (1, px), 1)
    pos_y = lane // res
    pos_x = lane % res

    def inside(oy, ox):
        ok_y = (pos_y + oy >= 0) & (pos_y + oy < res)
        ok_x = (pos_x + ox >= 0) & (pos_x + ox < res)
        return ok_y & ok_x

    def shift(value, oy, ox):
        steps = (-(oy * res + ox)) % px
        if steps == 0:
            return value
        return jnp.where(inside(oy, ox), pltpu.roll(value, steps, 1), 0.0)

    for m in range(mb):
        for op in gather_in(*of_sample(m)):
            op.wait_recv()
        x_all = xfull[:, pl.ds(pl.multiple_of((dp * mb + m) * px, px), px)]
        conv = jnp.zeros((ow, px), f32)
        for k, (oy, ox) in enumerate(OFFSETS):
            part = jnp.dot(wt[k * ow : (k + 1) * ow, :], x_all, preferred_element_type=f32)
            conv = conv + shift(part, oy, ox)
        pre = (
            demods[:, m : m + 1] * conv
            + cols[:, 4:5] * noise_ref[0, m : m + 1, :]
            + cols[:, 3:4]
        )
        act, slope = leaky_pair(pre)
        y = (root_two * act).astype(bf16)
        conv_s[m] = conv
        pre_s[m] = root_two * slope

        ytx[m] = y

        @pl.when(seg == 0)
        def _():
            y_copy(m).start()

        img[m, me_group] = jnp.dot(pack[...].astype(bf16), y, preferred_element_type=f32)[0:8]
        for j in range(1, ng):
            image_copy(m, j, me_group).start()

    for m in range(mb):
        for j in range(1, ng):
            image_copy(m, j, lax.rem(me_group + ng - j, ng)).wait_recv()
        total = img[m, 0]
        for g in range(1, ng):
            total = total + img[m, g]
        q = dcols[:, 3:4]
        for c in range(3):
            q = q + dcols[:, c : c + 1] * total[c : c + 1, :]
        act, slope = leaky_pair(q)
        out_col = dcols[:, 4:5]
        logit = jnp.sum(jnp.sum(act, axis=1, keepdims=True) * out_col, axis=0, keepdims=True) / px
        logit_out[m] = jnp.sum(logit)
        e = jnp.exp(-jnp.abs(logit))
        grad = jnp.where(logit >= 0.0, 1.0, e) / (1.0 + e) - 1.0
        dq = (grad * out_col / px) * slope
        for c in range(3):
            dimg[m, c : c + 1, :] = jnp.sum(dcols[:, c : c + 1] * dq, axis=0, keepdims=True)

    def forward_x():
        for jd in range(1, nd):
            for m in range(mb):
                x_dp_in(m, jd).wait_recv()
            for op in gather_out(*of_dp(jd)):
                op.start()

    @pl.when(seg == 0)
    def _():
        forward_x()

    coefall[dp] = jnp.zeros((coefall.shape[1], ow), f32)
    for m in range(mb):

        @pl.when(seg == 0)
        def _():
            ret_copy(m).wait_recv()

        dy = retbuf[m].astype(f32)
        for c in range(3):
            dy = dy + cols[:, c : c + 1] * dimg[m, c : c + 1, :]
        da = dy * pre_s[m]
        demod = demods[:, m : m + 1]
        gz = (da * demod).astype(bf16)
        gz_block(dp, m)[...] = gz
        for j in range(1, nd):
            gz_copy(m, j, dp).start()
        coef = -jnp.sum(da * conv_s[m], axis=1, keepdims=True) * demod * demod * demod
        wide = gz.astype(f32)
        for k, (oy, ox) in enumerate(OFFSETS):
            gst[m, k * ow : (k + 1) * ow, :] = shift(wide, -oy, -ox).astype(bf16)
        for j in range(1, nc):
            rows = pl.ds(pl.multiple_of(chan_peer(j) * ow, ow), ow)
            tx[m, j - 1] = jnp.dot(
                wcat[rows, :], gst[m], preferred_element_type=f32
            ).astype(bf16)
            dx_copy(m, j).start()
        rows = pl.ds(pl.multiple_of(ch * ow, ow), ow)
        dxown[m] = jnp.dot(wcat[rows, :], gst[m], preferred_element_type=f32)
        coefall[dp, m : m + 1, :] = jnp.broadcast_to(coef, (ow, ow)).T[0:1, :]

    for j in range(1, nd):
        coef_dp(j, dp).start()

    for m in range(mb):
        total = dxown[m]
        for j in range(1, nc):
            dx_copy(m, j).wait_recv()
            total = total + rx[m, j - 1].astype(f32)
        returned = (total * cols[:, 5 + m : 6 + m]).astype(bf16)
        ret_out[0, m] = returned
        rettx[m] = returned

        @pl.when(seg == 1)
        def _():
            ret_copy(m).start()

    @pl.when(seg == 1)
    def _():
        forward_x()

    for jd in range(1, nd):
        relay(of_dp(jd))

    rows_out = grad_out.shape[1]
    piece = math.gcd(rows_out, full)
    first_tap = (dp * rows_out) // full
    taps = gt.shape[0]
    for j in range(1, nd):
        for m in range(mb):
            gz_copy(m, j, dp_from(j)).wait_recv()
        style_dp(j, dp_from(j)).wait_recv()
        coef_dp(j, dp_from(j)).wait_recv()
    src = lax.broadcasted_iota(jnp.int32, (px, px), 0)
    dst = lax.broadcasted_iota(jnp.int32, (px, px), 1)
    dst_y, dst_x = dst // res, dst % res
    for t in range(taps):
        k = jnp.minimum(first_tap + t, 8)
        oy, ox = k // 3 - 1, lax.rem(k, 3) - 1
        ok_y = (dst_y - oy >= 0) & (dst_y - oy < res)
        ok_x = (dst_x - ox >= 0) & (dst_x - ox < res)
        hit = (src == dst - (oy * res + ox)) & ok_y & ok_x
        select = jnp.where(hit, 1.0, 0.0).astype(bf16)
        for b in range(nb):
            span = slice(b * px, (b + 1) * px)
            gt[t, :, span] = jnp.dot(
                gzall[:, span], select, preferred_element_type=f32
            ).astype(bf16)
    style_rows = jnp.concatenate([styall[d, 0:mb, :] for d in range(nd)], axis=0)
    style_cols = (style_rows * style_rows).T
    total = jnp.zeros((full, ow), f32)
    for b in range(nb):
        total = total + style_cols[:, b : b + 1] * coefall[b // mb, b % mb : b % mb + 1, :]
    dmat[...] = total
    for jd in range(1, nd):
        for op in gather_in(*of_dp(jd)):
            op.wait_recv()
    for r in range(rows_out // piece):
        start = dp * rows_out + r * piece
        t = start // full - first_tap
        inner = pl.ds(pl.multiple_of(lax.rem(start, full), piece), piece)
        prod = lax.dot_general(
            xfull[inner, :], gt[t], (((1,), (1,)), ((), ())), preferred_element_type=f32
        )
        weight = w_ref[0, pl.ds(pl.multiple_of(start, piece), piece), :].astype(f32)
        grad_out[0, r * piece : (r + 1) * piece, :] = prod + weight * dmat[inner, :]

    for m in range(mb):
        for op in gather_out(*of_sample(m)) + gather_relay(*of_sample(m)):
            op.wait_send()
        for j in range(1, nc):
            dx_copy(m, j).wait_send()
        for j in range(1, ng):
            image_copy(m, j, me_group).wait_send()
        for j in range(1, nd):
            x_dp(m, j).wait_send()
            gz_copy(m, j, dp).wait_send()
    for j in range(1, nd):
        style_dp(j, dp).wait_send()
        coef_dp(j, dp).wait_send()
        for op in gather_out(*of_dp(j)) + gather_relay(*of_dp(j)):
            op.wait_send()

    @pl.when(seg == 0)
    def _():
        for m in range(mb):
            y_copy(m).wait_send()

    @pl.when(seg == 1)
    def _():
        for m in range(mb):
            ret_copy(m).wait_send()


def shards(nd, nc, *args):
    base, style, noise, w, bias, gain, rgb, dw, db, do = args
    mb, ow, px = base.shape
    full = w.shape[1] // 9
    cd = dw.shape[1]
    nb = nd * mb
    rows_out = w.shape[1] // nd
    piece = math.gcd(rows_out, full)
    taps = max(
        ((d + 1) * rows_out - piece) // full - (d * rows_out) // full + 1 for d in range(nd)
    )
    mp = -(-mb // 8) * 8
    dma = pltpu.SemaphoreType.DMA
    pd, pc, pg = max(nd - 1, 1), max(nc - 1, 1), 2 * nc - 1
    vm = pltpu.VMEM
    prow = -(-(5 + mb) // 16) * 16
    scratch = [
        vm((prow, ow), f32),
        vm((ow, prow), f32),
        vm((8, cd), f32),
        vm((cd, 8), f32),
        vm((9 * ow, full), bf16),
        vm((full, 9 * ow), bf16),
        vm((ow, mp), f32),
        vm((mb, ow, px), bf16),
        vm((mb, ow, px), bf16),
        vm((full, nb * px), bf16),
        vm((nd, mp, full), f32),
        vm((nd, mp, ow), f32),
        vm((mb, ow, px), f32),
        vm((mb, ow, px), f32),
        vm((mb, 2 * nc, 8, px), f32),
        vm((mb, 8, px), f32),
        vm((ow, nb * px), bf16),
        vm((mb, 9 * ow, px), bf16),
        vm((mb, pc, ow, px), bf16),
        vm((mb, pc, ow, px), bf16),
        vm((mb, ow, px), f32),
        vm((mb, ow, px), bf16),
        vm((mb, ow, px), bf16),
        vm((taps, ow, nb * px), bf16),
        vm((full, ow), f32),
    ]
    for dims in ((mb, pc), (mb, pd), (pd, pc), (mb, pg), (mb,), (mb, pc), (mb,), (mb, pd), (pd,), (pd,)):
        scratch += [dma(dims), dma(dims)]
    spec = pl.BlockSpec(memory_space=pltpu.VMEM)
    return pl.pallas_call(
        functools.partial(kernel, nd, nc),
        out_shape=(
            jax.ShapeDtypeStruct((1, rows_out, ow), f32),
            jax.ShapeDtypeStruct((mb,), f32),
            jax.ShapeDtypeStruct((1, mb, ow, px), bf16),
        ),
        in_specs=[spec] * 10,
        out_specs=(spec, pl.BlockSpec(memory_space=pltpu.SMEM), spec),
        scratch_shapes=scratch,
        compiler_params=pltpu.CompilerParams(
            collective_id=0, has_side_effects=True, vmem_limit_bytes=56 * 1024 * 1024
        ),
    )(base, style, noise, w, bias, gain, rgb, dw, db[None, :], do[None, :])


def solution(mesh):
    placed = (
        P("dp", "chan", None),
        P("segment", "dp", None),
        P("segment", "dp", None),
        P("segment", None, "chan"),
        P("segment", "chan"),
        P("segment", "chan"),
        P("segment", None, "chan"),
        P(),
        P(),
        P(),
    )
    return jax.shard_map(
        functools.partial(shards, mesh.shape["dp"], mesh.shape["chan"]),
        mesh=mesh,
        in_specs=placed,
        out_specs=(P("segment", "dp", "chan"), P("dp"), P("segment", "dp", "chan", None)),
        check_vma=False,
    )
```

time: 227 us -> 57.5 us (0.25)
  waiting for transfers between devices: 87.5 us -> 0 us
  Pallas kernels: 0 us -> 53.6 us
  blocking collectives: 34.8 us -> 0 us
  other arithmetic: 29.1 us -> 0 us
  matrix products: 27.4 us -> 0 us
  local copies, waits for them, and re-layouts: 23.6 us -> 3.13 us
  between operations: 14.8 us -> 0.66 us
  starting transfers between devices: 8.37 us -> 0 us
    reduce_scatter x4 -> x0, waiting for transfers between devices: 83.5 us -> none  [the longest x3 53.8 us: shards(): d_input = lax.psum_scatter(total, 'chan', scatter_dimension=0, tiled=True)]
    pallas_call x0 -> x1, Pallas kernels: none -> 53.6 us  [shards(): pl.pallas_call(functools.partial(kernel, nd, nc), out_shape=(jax.ShapeDty...]
    dot_general x40 -> x0, matrix products: 27.4 us -> none  [the longest x27 8.59 us: shards(): lax.dot_general(weight_rows, d_conv, (((1,), (0,)), ((), ())), preferred_...]
    all_gather x3 -> x0, blocking collectives: 18.9 us -> none  [shards(): gathered = lax.all_gather(modulated, 'chan', axis=0, tiled=True)]
    dynamic_update_slice x10 -> x0, other arithmetic: 17.8 us -> none  [store_slot(): lax.dynamic_update_slice_in_dim(buffer, jnp.where(is_valid, item, previou...]
    psum x1 -> x0, blocking collectives: 16 us -> none  [shards(): images = lax.psum(image_part, ('segment', 'chan'))]
    ppermute x4 -> x0, starting transfers between devices: 8.21 us -> none  [shifted(): lax.ppermute(value, axis, [(source, source + steps) for source in range(f...]
    dynamic_slice x4 -> x0, local copies, waits for them, and re-layouts: 5.26 us -> none  [the longest x3 4.71 us: shards(): first_input = lax.dynamic_index_in_dim(base, slot_clip, 0, keepdims=False)]
  transfers between devices with their start and end apart: 8 -> 0, of which waited for: 7 -> 0; matrix products, arithmetic and copies ran while one was open for 12% -> 0% of each run, Pallas kernels for 0% -> 0%
where the time goes in v1:
time: 57.5 us; the launch traced here: 57.4 us
  Pallas kernels  53.6 us (93%)
  local copies, waits for them, and re-layouts  3.13 us (5%)
  between operations  0.66 us (1%)
    pallas_call x1, Pallas kernels, shards(): pl.pallas_call(functools.partial(kernel, nd, nc), out_shape=(jax.ShapeDty...  53.6 us
    unnamed x7, local copies, waits for them, and re-layouts  3.13 us

profile of v1, /device:TPU:0, one launch (start us, length us, event | category | flops | bytes accessed | tf_op | source)
XLA Modules:
  0.0 57.4 jit_solution(6469436528299709219)
XLA Ops:
  0.6 53.6 %shard_map.121 = (f32[1,1152,128]{2,1,0:T(8,128)}, f32[2]{0:T(128)}, bf16[1,2,128,256]{3,2,1,0:T(8,128)(2,1)}) custom-call(bf16[2,128,256]{2,1,0:T(8,128)(2,1)} %base_ref.1, f32[1,2,512]{2,1,0:T(2,128)} %style_ref.1, f32[1,2,256]{2,1,0:T(2,128)} %noise_ref.1, bf16[1,4608,128]{2,1,0:T(8,128)(2,1)} %w_ref.1, f32[1,128]{1,0:T(1,128)} %bias_ref.1, ...), custom_call_target="tpu_custom_call" | custom-call | tf_op jit(solution)/shard_map/pallas_call | solution.py:555
  54.2 0.0 copy-start.1
  54.3 0.0 copy-start
  54.3 2.0 %copy.16 = f32[1,1152,128]{2,1,0:T(8,128)} copy(f32[1,1152,128]{2,1,0:T(8,128)} %get-tuple-element.6) | data formatting | bytes 1179648
  56.2 0.0 copy-done.1
  56.2 0.5 copy.17
  56.7 0.0 copy-done
  56.7 0.7 %copy.18 = bf16[1,2,128,256]{3,2,1,0:T(8,128)(2,1)} copy(bf16[1,2,128,256]{3,2,1,0:T(8,128)(2,1)S(1)} %copy-done) | data formatting | bytes 262144
Async XLA Ops:
  54.2 2.0 %copy-start.1 = (f32[2]{0:T(128)S(1)}, f32[2]{0:T(128)}, u32[]{:S(2)}) copy-start(f32[2]{0:T(128)} %get-tuple-element.7) | copy-start | bytes 28
  54.3 2.5 %copy-start = (bf16[1,2,128,256]{3,2,1,0:T(8,128)(2,1)S(1)}, bf16[1,2,128,256]{3,2,1,0:T(8,128)(2,1)}, u32[]{:S(2)}) copy-start(bf16[1,2,128,256]{3,2,1,0:T(8,128)(2,1)} %get-tuple-element.8) | copy-start | bytes 393220

commit v2 on v1

--- a/solution.py
+++ b/solution.py
@@ -74,6 +74,7 @@
     rettx,
     gt,
     dmat,
+    sel,
     xg_s,
     xg_r,
     xd_s,
@@ -236,13 +237,10 @@
     def ret_copy(m):
         return remote(rettx.at[m], retbuf.at[m], rt_s.at[m], rt_r.at[m], at(dp, 1 - seg, ch))
 
-    def dx_copy(m, j):
+    def dx_copy(m, i):
+        dev = other if i < pairs else same_core(i - pairs + 1)
         return remote(
-            tx.at[m, j - 1],
-            rx.at[m, j - 1],
-            rs_s.at[m, j - 1],
-            rs_r.at[m, j - 1],
-            at(dp, seg, chan_peer(j)),
+            tx.at[m, i], rx.at[m, i], rs_s.at[m, i], rs_r.at[m, i], at(dp, seg, dev)
         )
 
     def gz_block(d, m):
@@ -372,6 +370,22 @@
         for c in range(3):
             dimg[m, c : c + 1, :] = jnp.sum(dcols[:, c : c + 1] * dq, axis=0, keepdims=True)
 
+    rows_out = grad_out.shape[1]
+    first_tap = (dp * rows_out) // full
+    taps = gt.shape[0]
+
+    def make_selects():
+        src = lax.broadcasted_iota(jnp.int32, (px, px), 0)
+        dst = lax.broadcasted_iota(jnp.int32, (px, px), 1)
+        dst_y, dst_x = dst // res, dst % res
+        for t in range(taps):
+            k = jnp.minimum(first_tap + t, 8)
+            oy, ox = k // 3 - 1, lax.rem(k, 3) - 1
+            ok_y = (dst_y - oy >= 0) & (dst_y - oy < res)
+            ok_x = (dst_x - ox >= 0) & (dst_x - ox < res)
+            hit = (src == dst - (oy * res + ox)) & ok_y & ok_x
+            sel[t] = jnp.where(hit, 1.0, 0.0).astype(bf16)
+
     def forward_x():
         for jd in range(1, nd):
             for m in range(mb):
@@ -382,6 +396,7 @@
     @pl.when(seg == 0)
     def _():
         forward_x()
+        make_selects()
 
     coefall[dp] = jnp.zeros((coefall.shape[1], ow), f32)
     for m in range(mb):
@@ -403,14 +418,23 @@
         wide = gz.astype(f32)
         for k, (oy, ox) in enumerate(OFFSETS):
             gst[m, k * ow : (k + 1) * ow, :] = shift(wide, -oy, -ox).astype(bf16)
-        for j in range(1, nc):
-            rows = pl.ds(pl.multiple_of(chan_peer(j) * ow, ow), ow)
-            tx[m, j - 1] = jnp.dot(
-                wcat[rows, :], gst[m], preferred_element_type=f32
-            ).astype(bf16)
-            dx_copy(m, j).start()
-        rows = pl.ds(pl.multiple_of(ch * ow, ow), ow)
-        dxown[m] = jnp.dot(wcat[rows, :], gst[m], preferred_element_type=f32)
+
+        def part(c):
+            rows = pl.ds(pl.multiple_of(c * ow, ow), ow)
+            return jnp.dot(wcat[rows, :], gst[m], preferred_element_type=f32)
+
+        for q in range(1, pairs):
+            tx[m, q] = part(lax.rem(pair + q, pairs) * 2 + 1 - core).astype(bf16)
+            dx_copy(m, q).start()
+        mine = [part(same_core(q)) for q in range(1, pairs)]
+        tx[m, 0] = part(other).astype(bf16)
+        dx_copy(m, 0).start()
+        dxown[m] = part(ch)
+        for q in range(1, pairs):
+            i = pairs - 1 + q
+            dx_copy(m, q).wait_recv()
+            tx[m, i] = (mine[q - 1] + rx[m, q].astype(f32)).astype(bf16)
+            dx_copy(m, i).start()
         coefall[dp, m : m + 1, :] = jnp.broadcast_to(coef, (ow, ow)).T[0:1, :]
 
     for j in range(1, nd):
@@ -418,9 +442,9 @@
 
     for m in range(mb):
         total = dxown[m]
-        for j in range(1, nc):
-            dx_copy(m, j).wait_recv()
-            total = total + rx[m, j - 1].astype(f32)
+        for i in [0] + list(range(pairs, nc - 1)):
+            dx_copy(m, i).wait_recv()
+            total = total + rx[m, i].astype(f32)
         returned = (total * cols[:, 5 + m : 6 + m]).astype(bf16)
         ret_out[0, m] = returned
         rettx[m] = returned
@@ -432,34 +456,24 @@
     @pl.when(seg == 1)
     def _():
         forward_x()
+        make_selects()
 
     for jd in range(1, nd):
         relay(of_dp(jd))
 
-    rows_out = grad_out.shape[1]
     piece = math.gcd(rows_out, full)
-    first_tap = (dp * rows_out) // full
-    taps = gt.shape[0]
+    for m in range(mb):
+        for j in range(nd):
+            if j > 0:
+                gz_copy(m, j, dp_from(j)).wait_recv()
+            span = pl.ds(pl.multiple_of((dp_from(j) * mb + m) * px, px), px)
+            for t in range(taps):
+                gt[t, :, span] = jnp.dot(
+                    gzall[:, span], sel[t], preferred_element_type=f32
+                ).astype(bf16)
     for j in range(1, nd):
-        for m in range(mb):
-            gz_copy(m, j, dp_from(j)).wait_recv()
         style_dp(j, dp_from(j)).wait_recv()
         coef_dp(j, dp_from(j)).wait_recv()
-    src = lax.broadcasted_iota(jnp.int32, (px, px), 0)
-    dst = lax.broadcasted_iota(jnp.int32, (px, px), 1)
-    dst_y, dst_x = dst // res, dst % res
-    for t in range(taps):
-        k = jnp.minimum(first_tap + t, 8)
-        oy, ox = k // 3 - 1, lax.rem(k, 3) - 1
-        ok_y = (dst_y - oy >= 0) & (dst_y - oy < res)
-        ok_x = (dst_x - ox >= 0) & (dst_x - ox < res)
-        hit = (src == dst - (oy * res + ox)) & ok_y & ok_x
-        select = jnp.where(hit, 1.0, 0.0).astype(bf16)
-        for b in range(nb):
-            span = slice(b * px, (b + 1) * px)
-            gt[t, :, span] = jnp.dot(
-                gzall[:, span], select, preferred_element_type=f32
-            ).astype(bf16)
     style_rows = jnp.concatenate([styall[d, 0:mb, :] for d in range(nd)], axis=0)
     style_cols = (style_rows * style_rows).T
     total = jnp.zeros((full, ow), f32)
@@ -482,8 +496,8 @@
     for m in range(mb):
         for op in gather_out(*of_sample(m)) + gather_relay(*of_sample(m)):
             op.wait_send()
-        for j in range(1, nc):
-            dx_copy(m, j).wait_send()
+        for i in range(nc - 1):
+            dx_copy(m, i).wait_send()
         for j in range(1, ng):
             image_copy(m, j, me_group).wait_send()
         for j in range(1, nd):
@@ -548,6 +562,7 @@
         vm((mb, ow, px), bf16),
         vm((taps, ow, nb * px), bf16),
         vm((full, ow), f32),
+        vm((taps, px, px), bf16),
     ]
     for dims in ((mb, pc), (mb, pd), (pd, pc), (mb, pg), (mb,), (mb, pc), (mb,), (mb, pd), (pd,), (pd,)):
         scratch += [dma(dims), dma(dims)]

time: 57.5 us -> 56.8 us (0.988)
  Pallas kernels: 53.6 us -> 52.8 us
    pallas_call x1, Pallas kernels: 53.6 us -> 52.8 us  [shards(): pl.pallas_call(functools.partial(kernel, nd, nc), out_shape=(jax.ShapeDty...]
where the time goes in v2:
time: 56.8 us; the launch traced here: 56.6 us
  Pallas kernels  52.8 us (93%)
  local copies, waits for them, and re-layouts  3.13 us (6%)
  between operations  0.66 us (1%)
    pallas_call x1, Pallas kernels, shards(): pl.pallas_call(functools.partial(kernel, nd, nc), out_shape=(jax.ShapeDty...  52.8 us
    unnamed x7, local copies, waits for them, and re-layouts  3.13 us

profile of v2, /device:TPU:0, one launch (start us, length us, event | category | flops | bytes accessed | tf_op | source)
XLA Modules:
  0.0 56.6 jit_solution(584937057239108893)
XLA Ops:
  0.6 52.8 %shard_map.121 = (f32[1,1152,128]{2,1,0:T(8,128)}, f32[2]{0:T(128)}, bf16[1,2,128,256]{3,2,1,0:T(8,128)(2,1)}) custom-call(bf16[2,128,256]{2,1,0:T(8,128)(2,1)} %base_ref.1, f32[1,2,512]{2,1,0:T(2,128)} %style_ref.1, f32[1,2,256]{2,1,0:T(2,128)} %noise_ref.1, bf16[1,4608,128]{2,1,0:T(8,128)(2,1)} %w_ref.1, f32[1,128]{1,0:T(1,128)} %bias_ref.1, ...), custom_call_target="tpu_custom_call" | custom-call | tf_op jit(solution)/shard_map/pallas_call | solution.py:570
  53.5 0.0 copy-start.1
  53.5 0.0 copy-start
  53.5 2.0 %copy.16 = f32[1,1152,128]{2,1,0:T(8,128)} copy(f32[1,1152,128]{2,1,0:T(8,128)} %get-tuple-element.6) | data formatting | bytes 1179648
  55.5 0.0 copy-done.1
  55.5 0.5 copy.17
  56.0 0.0 copy-done
  56.0 0.7 %copy.18 = bf16[1,2,128,256]{3,2,1,0:T(8,128)(2,1)} copy(bf16[1,2,128,256]{3,2,1,0:T(8,128)(2,1)S(1)} %copy-done) | data formatting | bytes 262144
Async XLA Ops:
  53.5 2.0 %copy-start.1 = (f32[2]{0:T(128)S(1)}, f32[2]{0:T(128)}, u32[]{:S(2)}) copy-start(f32[2]{0:T(128)} %get-tuple-element.7) | copy-start | bytes 28
  53.5 2.5 %copy-start = (bf16[1,2,128,256]{3,2,1,0:T(8,128)(2,1)S(1)}, bf16[1,2,128,256]{3,2,1,0:T(8,128)(2,1)}, u32[]{:S(2)}) copy-start(bf16[1,2,128,256]{3,2,1,0:T(8,128)(2,1)} %get-tuple-element.8) | copy-start | bytes 393220
